TPU v7x, 32 devices: a whole 2x2x4 slice. The times are simulated.
32 devices in a mesh: wide: 8 (over y, x, core), narrow: 4 (over z).
Axes of the slice: x: 2, y: 2, z: 4, core: 2. Of those that a mesh axis runs over, the one named last changes fastest.
Arguments:
- control: float32 [64, 512, 1024], P(None, 'wide', 'narrow'), may hold values from -6 to 6
- length_scale: float32 [64], replicated, may hold values from 2 to 8
- modes: float32 [127, 64], replicated, may hold values from -0.75 to 0.75
- jacobian: float32 [128, 127], replicated, may hold values from -0.5 to 0.5
- obs_weight: float32 [128], replicated, may hold values from 0.2 to 5
- departures: float32 [8, 4, 8, 128, 128], P('wide', 'narrow'), may hold values from -6 to 6
- send_cols: int32 [8, 4, 8, 128], P('wide', 'narrow'), may hold values from 0 to 16383
- counts: int32 [8, 4, 8], P('wide', 'narrow'), may hold values from 1 to 128, as said below
Outputs:
- gradient: float32 [64, 512, 1024], P(None, 'wide', 'narrow')
- obs_residual: float32 [8, 4, 8, 128, 128], P('wide', 'narrow')
Inputs may be any that keep to these rules, and one draw needn't show every extreme that they name: counts[s, b, o] live slots from the device at longitude tile s and latitude tile b to owner o; in every draw one owner receives 128 from every source. `send_cols`: a local column index of the source device, with latitude varying fastest: i * 256 + j, where i is the local longitude row and j the local latitude column.
All inputs are finite; a program needn't handle non-finite values.
Results may differ from a plain program's by a relative error of at most 0.00008.
Values sent between devices are 32-bit elements; how exact they have to be, the bound alone decides.
A program may use at most 128 MiB of HBM per device.

v0:
```python
import functools

import jax
import jax.numpy as jnp
from jax import lax
from jax.experimental import pallas as pl
from jax.experimental.pallas import tpu as pltpu
from jax.sharding import PartitionSpec as P

HALO = 15
REACH = 16
LANES = 128
STEP = 8
HIGHEST = lax.Precision.HIGHEST
VMEM_BYTES = 48 * 2**20


def split(x):
    high = x.astype(jnp.bfloat16)
    return high, (x - high.astype(jnp.float32)).astype(jnp.bfloat16)


def taps(offset, rate, scale):
    curve = jnp.exp((offset * offset).astype(jnp.float32) * rate) * scale
    return jnp.where(jnp.abs(offset) <= HALO, curve, 0.0)


def lon_kernel(halves, rate_ref, scale_ref, x_ref, before_ref, after_ref, y_ref, first_ref, last_ref):
    lon = y_ref.shape[1]
    depth = lon + 2 * REACH
    row = lax.broadcasted_iota(jnp.int32, (lon, depth), 0)
    col = lax.broadcasted_iota(jnp.int32, (lon, depth), 1)
    offset = col - REACH - row
    lane = lax.broadcasted_iota(jnp.int32, (8, LANES), 1)
    for m in range(STEP):
        mode = pl.program_id(0) * STEP + m
        if halves:
            x = jnp.concatenate([x_ref[0, m], x_ref[1, m]], axis=1)
            before = jnp.concatenate([before_ref[0, m], before_ref[1, m]], axis=1)
            after = jnp.concatenate([after_ref[0, m], after_ref[1, m]], axis=1)
        else:
            x, before, after = x_ref[m], before_ref[m], after_ref[m]
        high, low = split(jnp.concatenate([before, x, after], axis=0))
        w_high, w_low = split(taps(offset, rate_ref[mode], scale_ref[mode]))
        both = jnp.dot(
            jnp.concatenate([w_high, w_low], axis=0), high, preferred_element_type=jnp.float32
        )
        y = both[:lon] + both[lon:]
        y = y + jnp.dot(w_high, low, preferred_element_type=jnp.float32)
        y_ref[m] = y
        width = y.shape[1]
        first = jnp.zeros((8, LANES), jnp.float32)
        last = jnp.zeros((8, LANES), jnp.float32)
        for g in range(lon // 8):
            here = lane // REACH == g
            start = y[8 * g : 8 * g + 8, :LANES]
            end = y[8 * g : 8 * g + 8, width - LANES :]
            if g:
                start = pltpu.roll(start, REACH * g, 1)
            if g < lon // 8 - 1:
                end = pltpu.roll(end, (REACH * g + REACH) % LANES, 1)
            first = jnp.where(here, start, first)
            last = jnp.where(here, end, last)
        first_ref[m] = first
        last_ref[m] = last


def lat_kernel(add, rate_ref, scale_ref, y_ref, before_ref, after_ref, *rest):
    lon, lat = y_ref.shape[1], y_ref.shape[2]
    tiles = lat // LANES
    depth = 2 * LANES
    row = lax.broadcasted_iota(jnp.int32, (depth, LANES), 0)
    col = lax.broadcasted_iota(jnp.int32, (depth, LANES), 1)
    offset = jnp.where(row < 3 * LANES // 2, row, row - depth) - col
    near = lax.broadcasted_iota(jnp.int32, (lon, LANES), 1) < LANES // 2
    out_ref = rest[-1]
    for m in range(STEP):
        mode = pl.program_id(0) * STEP + m
        before, after = before_ref[m], after_ref[m]
        lefts, rights = [], []
        for g in range(lon // 8):
            lefts.append(pltpu.roll(before, LANES - REACH - REACH * g, 1) if g < 7 else before)
            rights.append(pltpu.roll(after, LANES - REACH * g, 1) if g else after)
        blocks = [y_ref[m, :, LANES * t : LANES * t + LANES] for t in range(tiles)]
        around = [jnp.concatenate(lefts, axis=0)] + blocks + [jnp.concatenate(rights, axis=0)]
        sides = [jnp.where(near, around[t + 2], around[t]) for t in range(tiles)]
        field = jnp.concatenate(
            [jnp.concatenate([blocks[t], sides[t]], axis=1) for t in range(tiles)], axis=0
        )
        high, low = split(field)
        w_high, w_low = split(taps(offset, rate_ref[mode], scale_ref[mode]))
        both = jnp.dot(
            jnp.concatenate([high, low], axis=0),
            jnp.concatenate([w_high, w_low], axis=1),
            preferred_element_type=jnp.float32,
        )
        count = tiles * lon
        z = both[:count, :LANES] + both[:count, LANES:] + both[count:, :LANES]
        for t in range(tiles):
            part = z[lon * t : lon * t + lon]
            if add:
                at = slice(LANES * t, LANES * t + LANES)
                out_ref[m, :, at] = rest[0][m, :, at] + part
            else:
                out_ref[t, m * lon : m * lon + lon, :] = part


def observe_kernel(lon, rows_ref, counts_ref, cols_ref, field_ref, normal_ref, offset_ref,
                   picked_ref, collected_ref, table, values):
    modes = normal_ref.shape[0]
    owners, slots = cols_ref.shape

    def to_table(i, carry):
        slab = jnp.concatenate(
            [field_ref[0, pl.ds(i, modes, stride=lon), :], field_ref[1, pl.ds(i, modes, stride=lon), :]],
            axis=0,
        )
        table[pl.ds(pl.multiple_of(i * LANES, LANES), LANES), :] = slab.T
        return carry

    lax.fori_loop(0, lon, to_table, 0, unroll=2)

    def pick(n, carry):
        for u in range(16):
            s = n * 16 + u
            values[pl.ds(s, 1), :] = table[pl.ds(rows_ref[s], 1), :]
        return carry

    lax.fori_loop(0, owners * slots // 16, pick, 0)
    table[...] = jnp.zeros_like(table)
    slot = lax.broadcasted_iota(jnp.int32, (modes, slots), 1)

    def respond(o, carry):
        at = pl.ds(pl.multiple_of(o * slots, slots), slots)
        both = values[at, :].T
        upper = (cols_ref[pl.ds(o, 1), :] & LANES) != 0
        picked = jnp.where(upper, both[modes:], both[:modes])
        count = counts_ref[o]
        picked_ref[o, :modes] = picked
        picked_ref[o, modes:] = jnp.full((8, slots), count.astype(jnp.float32))
        adjoint = jnp.dot(
            normal_ref[...], picked, precision=HIGHEST, preferred_element_type=jnp.float32
        ) - offset_ref[o]
        adjoint = jnp.where(slot < count, adjoint, 0.0)
        values[at, :] = jnp.concatenate(
            [jnp.where(upper, 0.0, adjoint), jnp.where(upper, adjoint, 0.0)], axis=0
        ).T
        return carry

    lax.fori_loop(0, owners, respond, 0)

    def collect(n, carry):
        for u in range(16):
            s = n * 16 + u
            row = rows_ref[s]
            table[pl.ds(row, 1), :] = table[pl.ds(row, 1), :] + values[pl.ds(s, 1), :]
        return carry

    lax.fori_loop(0, owners * slots // 16, collect, 0)

    def from_table(i, carry):
        slab = table[pl.ds(pl.multiple_of(i * LANES, LANES), LANES), :].T
        collected_ref[0, pl.ds(i, modes, stride=lon), :] = slab[:modes]
        collected_ref[1, pl.ds(i, modes, stride=lon), :] = slab[modes:]
        return carry

    lax.fori_loop(0, lon, from_table, 0, unroll=2)


SMEM = pl.BlockSpec(memory_space=pltpu.SMEM)


def by_mode(shape, dim=0):
    block = tuple(STEP if d == dim else n for d, n in enumerate(shape))
    return pl.BlockSpec(block, lambda g: tuple(g if d == dim else 0 for d in range(len(shape))))


def from_neighbours(axis, first, last):
    count = lax.axis_size(axis)
    up = [(i, i + 1) for i in range(count - 1)]
    down = [(j, i) for i, j in up]
    return lax.ppermute(last, axis, up), lax.ppermute(first, axis, down)


def along_lon(x, rate, scale, shape):
    modes, lon, lat = shape
    halves = x.ndim == 4
    dim = x.ndim - 2
    before, after = from_neighbours(
        "wide",
        lax.slice_in_dim(x, 0, REACH, axis=dim),
        lax.slice_in_dim(x, lon - REACH, lon, axis=dim),
    )
    at = 1 if halves else 0
    return pl.pallas_call(
        functools.partial(lon_kernel, halves),
        grid=(modes // STEP,),
        in_specs=[SMEM, SMEM, by_mode(x.shape, at), by_mode(before.shape, at), by_mode(after.shape, at)],
        out_specs=[by_mode(shape), by_mode((modes, 8, LANES)), by_mode((modes, 8, LANES))],
        out_shape=[
            jax.ShapeDtypeStruct(shape, jnp.float32),
            jax.ShapeDtypeStruct((modes, 8, LANES), jnp.float32),
            jax.ShapeDtypeStruct((modes, 8, LANES), jnp.float32),
        ],
        compiler_params=pltpu.CompilerParams(vmem_limit_bytes=VMEM_BYTES),
        name="along_lon",
    )(rate, scale, x, before, after)


def along_lat(y, first, last, rate, scale, added=None):
    modes, lon, lat = y.shape
    before, after = from_neighbours("narrow", first, last)
    extra = () if added is None else (added,)
    if added is None:
        out_shape = (lat // LANES, modes * lon, LANES)
        out_spec = pl.BlockSpec((lat // LANES, STEP * lon, LANES), lambda g: (0, g, 0))
    else:
        out_shape = y.shape
        out_spec = by_mode(y.shape)
    return pl.pallas_call(
        functools.partial(lat_kernel, added is not None),
        grid=(modes // STEP,),
        in_specs=[SMEM, SMEM, by_mode(y.shape), by_mode(before.shape), by_mode(after.shape)]
        + [by_mode(y.shape)] * len(extra),
        out_specs=out_spec,
        out_shape=jax.ShapeDtypeStruct(out_shape, jnp.float32),
        compiler_params=pltpu.CompilerParams(vmem_limit_bytes=VMEM_BYTES),
        name="along_lat",
    )(rate, scale, y, before, after, *extra)


def shards(control, length_scale, modes, jacobian, obs_weight, departures, send_cols, counts):
    owners = lax.axis_size("wide")
    shape = control.shape
    mode_count, lon, lat = shape
    channels = jacobian.shape[0]
    slots = send_cols.shape[-1]
    tiles = lat // LANES

    offsets = jnp.arange(-HALO, HALO + 1).astype(jnp.float32)
    total = jnp.sum(jnp.exp(-(offsets[None, :] ** 2) / length_scale[:, None] ** 2), axis=1)
    rate = -0.5 / (length_scale * length_scale)
    scale = 1.0 / jnp.sqrt(total)

    forward = jnp.dot(jacobian, modes, precision=HIGHEST)
    weighted = obs_weight[:, None] * forward
    normal = jnp.dot(forward.T, weighted, precision=HIGHEST)
    observed = departures.reshape(owners, channels, slots)
    projected = jnp.einsum("cm,sck->smk", weighted, observed, precision=HIGHEST)
    offset = lax.all_to_all(projected, "wide", split_axis=0, concat_axis=0, tiled=True)

    columns = send_cols.reshape(owners, slots)
    rows = ((columns // lat) * LANES + columns % LANES).reshape(-1)

    y, first, last = along_lon(control, rate, scale, shape)
    smoothed = along_lat(y, first, last, rate, scale)
    whole = pl.BlockSpec(memory_space=pltpu.VMEM)
    outgoing, collected = pl.pallas_call(
        functools.partial(observe_kernel, lon),
        in_specs=[SMEM, SMEM] + [whole] * 4,
        out_specs=[whole, whole],
        out_shape=[
            jax.ShapeDtypeStruct((owners, mode_count + 8, slots), jnp.float32),
            jax.ShapeDtypeStruct((tiles, mode_count * lon, LANES), jnp.float32),
        ],
        scratch_shapes=[
            pltpu.VMEM((lon * LANES, LANES), jnp.float32),
            pltpu.VMEM((owners * slots, LANES), jnp.float32),
        ],
        compiler_params=pltpu.CompilerParams(vmem_limit_bytes=VMEM_BYTES),
        name="observe",
    )(rows, counts.reshape(owners), columns, smoothed, normal, offset)

    y, first, last = along_lon(
        collected.reshape(tiles, mode_count, lon, LANES), rate, scale, shape
    )
    arrived = lax.all_to_all(outgoing, "wide", split_axis=0, concat_axis=0, tiled=True)
    gradient = along_lat(y, first, last, rate, scale, control)

    evolved = jnp.einsum("cm,smk->sck", forward, arrived[:, :mode_count], precision=HIGHEST)
    live = jnp.arange(slots).astype(jnp.float32) < arrived[:, mode_count, :]
    residual = jnp.where(
        live[:, None, :], obs_weight[None, :, None] * (evolved - observed), jnp.float32(0.0)
    )
    return (gradient, residual.reshape(departures.shape))


def solution(mesh):
    in_specs = (
        P(None, "wide", "narrow"),
        P(),
        P(),
        P(),
        P(),
        P("wide", "narrow", None, None, None),
        P("wide", "narrow", None, None),
        P("wide", "narrow", None),
    )
    out_specs = (P(None, "wide", "narrow"), P("wide", "narrow", None, None, None))
    return jax.shard_map(shards, mesh=mesh, in_specs=in_specs, out_specs=out_specs, check_vma=False)
```

profile of v0, /device:TPU:1, one launch (start us, length us, event | category | flops | bytes accessed | tf_op | source)
XLA Modules:
  0.0 144.9 jit_solution(13362254337470850659)
XLA Ops:
  0.7 3.1 %fusion.19 = (f32[64,16,256]{2,1,0:T(8,128)}, f32[64,16,256]{2,1,0:T(8,128)}) fusion(f32[64,64,256]{2,1,0:T(8,128)} %rest_0_.1), kind=kLoop, calls=%fused_computation.36 | loop fusion | bytes 4194304 | tf_op jit(solution)/shard_map/slice | solution.py:191
  3.8 4.6 %collective-permute-start = (f32[64,16,256]{2,1,0:T(8,128)}, f32[64,16,256]{2,1,0:T(8,128)S(1)}, u32[]{:S(2)}, u32[]{:S(2)}) collective-permute-start(f32[64,16,256]{2,1,0:T(8,128)} %get-tuple-element.27), channel_id=1, source_target_pairs={{0,4},{4,8},{8,12},{12,16},{16,20},{20,24},{24,28},{1,5},{5,9},{9,... | collective-permute-start | bytes 3145736 | tf_op jit(solution)/shard_map/ppermute | solution.py:182
  8.5 1.9 %collective-permute-start.1 = (f32[64,16,256]{2,1,0:T(8,128)}, f32[64,16,256]{2,1,0:T(8,128)S(1)}, u32[]{:S(2)}, u32[]{:S(2)}) collective-permute-start(f32[64,16,256]{2,1,0:T(8,128)} %get-tuple-element.26), channel_id=1, source_target_pairs={{4,0},{8,4},{12,8},{16,12},{20,16},{24,20},{28,24},{5,1},{9,5},{13... | collective-permute-start | bytes 3145736 | tf_op jit(solution)/shard_map/ppermute | solution.py:182
  10.4 0.2 fusion.20
  10.7 1.1 convolution_bitcast_fusion.1
  11.8 4.4 %all-to-all-start = ((f32[8,64,128]{2,1,0:T(8,128)}), f32[8,64,128]{2,1,0:T(8,128)S(1)}, u32[]{:S(2)}, u32[]{:S(2)}) async-start(f32[8,64,128]{2,1,0:T(8,128)} %convolution_bitcast_fusion.1), calls=%async_computation | async-start | bytes 524288 | tf_op jit(solution)/shard_map/all_to_all | solution.py:250
  16.3 5.6 %collective-permute-done.before_ref = f32[64,16,256]{2,1,0:T(8,128)S(1)} collective-permute-done((f32[64,16,256]{2,1,0:T(8,128)}, f32[64,16,256]{2,1,0:T(8,128)S(1)}, u32[]{:S(2)}, u32[]{:S(2)}) %collective-permute-start) | collective-permute-done | bytes 1048608 | tf_op jit(solution)/shard_map/ppermute | solution.py:182
  21.9 13.1 %collective-permute-done.1.after_ref = f32[64,16,256]{2,1,0:T(8,128)S(1)} collective-permute-done((f32[64,16,256]{2,1,0:T(8,128)}, f32[64,16,256]{2,1,0:T(8,128)S(1)}, u32[]{:S(2)}, u32[]{:S(2)}) %collective-permute-start.1) | collective-permute-done | bytes 1048608 | tf_op jit(solution)/shard_map/ppermute | solution.py:182
  35.0 7.8 %along_lon.2 = (f32[64,64,256]{2,1,0:T(8,128)}, f32[64,8,128]{2,1,0:T(8,128)S(1)}, f32[64,8,128]{2,1,0:T(8,128)S(1)}) custom-call(f32[64]{0:T(128)S(1)} %get-tuple-element.28.rate_ref, f32[64]{0:T(128)S(1)} %sqrt.3.scale_ref, f32[64,64,256]{2,1,0:T(8,128)} %rest_0_.1, f32[64,16,256]{2,1,0:T(8,128)S(1)} %collective-permute-done.before_ref, ...), custom_call_target="tpu_custom_call" | custom-call | tf_op jit(solution)/shard_map/along_lon/pallas_call | solution.py:195
  42.8 3.2 %collective-permute-start.2 = (f32[64,8,128]{2,1,0:T(8,128)S(1)}, f32[64,8,128]{2,1,0:T(8,128)S(1)}, u32[]{:S(2)}, u32[]{:S(2)}) collective-permute-start(f32[64,8,128]{2,1,0:T(8,128)S(1)} %get-tuple-element.11), channel_id=1, source_target_pairs={{0,1},{1,2},{2,3},{4,5},{5,6},{6,7},{8,9},{9,10},{10,11},{12,13},{... | collective-permute-start | bytes 786440 | tf_op jit(solution)/shard_map/ppermute | solution.py:182
  46.0 1.3 collective-permute-start.3
  47.5 1.8 %collective-permute-done.2.before_ref = f32[64,8,128]{2,1,0:T(8,128)S(1)} collective-permute-done((f32[64,8,128]{2,1,0:T(8,128)S(1)}, f32[64,8,128]{2,1,0:T(8,128)S(1)}, u32[]{:S(2)}, u32[]{:S(2)}) %collective-permute-start.2) | collective-permute-done | bytes 262176 | tf_op jit(solution)/shard_map/ppermute | solution.py:182
  49.3 3.8 %collective-permute-done.3.after_ref = f32[64,8,128]{2,1,0:T(8,128)S(1)} collective-permute-done((f32[64,8,128]{2,1,0:T(8,128)S(1)}, f32[64,8,128]{2,1,0:T(8,128)S(1)}, u32[]{:S(2)}, u32[]{:S(2)}) %collective-permute-start.3) | collective-permute-done | bytes 262176 | tf_op jit(solution)/shard_map/ppermute | solution.py:182
  53.1 7.6 %along_lat.2.field_ref = f32[2,4096,128]{2,1,0:T(8,128)S(1)} custom-call(f32[64]{0:T(128)S(1)} %get-tuple-element.28.rate_ref, f32[64]{0:T(128)S(1)} %sqrt.3.scale_ref, f32[64,64,256]{2,1,0:T(8,128)} %get-tuple-element.10.y_ref, f32[64,8,128]{2,1,0:T(8,128)S(1)} %collective-permute-done.2.before_ref, f32[64,8,128]{2,1,0:T(8,128)S(1)} %collective-permute-done.3.after_ref), custom_call_target="tpu_custom_call" | custom-call | tf_op jit(solution)/shard_map/along_lat/pallas_call | solution.py:220
  60.7 2.0 %copy-done.1 = f32[2,4096,128]{2,1,0:T(8,128)} copy-done((f32[2,4096,128]{2,1,0:T(8,128)}, f32[2,4096,128]{2,1,0:T(8,128)S(1)}, u32[]{:S(2)}) %copy-start.1) | copy-done | bytes 4194328
  62.8 18.9 %observe.1 = (f32[8,72,128]{2,1,0:T(8,128)}, f32[2,4096,128]{2,1,0:T(8,128)S(1)}) custom-call(s32[1024]{0:T(1024)S(1)} %fusion.14.rows_ref, s32[8]{0:T(128)S(1)} %bitcast.63, s32[8,128]{1,0:T(8,128)S(1)} %bitcast.62, f32[2,4096,128]{2,1,0:T(8,128)} %copy-done.1, f32[64,64]{1,0:T(8,128)S(1)} %fusion.6.normal_ref, f32[8,64,128]{2,1,0:T(8,128)S(1)} %all-to-all-done.offset_ref), custom_call_target="tpu_custom_call" | custom-call | tf_op jit(solution)/shard_map/observe/pallas_call | solution.py:258
  81.7 2.0 %copy-done.2 = f32[2,4096,128]{2,1,0:T(8,128)} copy-done((f32[2,4096,128]{2,1,0:T(8,128)}, f32[2,4096,128]{2,1,0:T(8,128)S(1)}, u32[]{:S(2)}) %copy-start.2) | copy-done | bytes 4194328
  83.7 1.5 %fusion.18 = (f32[2,64,16,128]{3,2,1,0:T(8,128)}, f32[2,64,16,128]{3,2,1,0:T(8,128)}) fusion(f32[2,64,64,128]{3,2,1,0:T(8,128)S(1)} %bitcast.60), kind=kLoop, calls=%fused_computation.35 | loop fusion | bytes 4194304 | tf_op jit(solution)/shard_map/slice | solution.py:191
  85.2 5.5 %collective-permute-start.4 = (f32[2,64,16,128]{3,2,1,0:T(8,128)}, f32[2,64,16,128]{3,2,1,0:T(8,128)S(1)}, u32[]{:S(2)}, u32[]{:S(2)}) collective-permute-start(f32[2,64,16,128]{3,2,1,0:T(8,128)} %get-tuple-element.25), channel_id=1, source_target_pairs={{0,4},{4,8},{8,12},{12,16},{16,20},{20,24},{24,28},{1,5},{5,9},{9,... | collective-permute-start | bytes 3145736 | tf_op jit(solution)/shard_map/ppermute | solution.py:182
  90.7 1.9 %collective-permute-start.5 = (f32[2,64,16,128]{3,2,1,0:T(8,128)}, f32[2,64,16,128]{3,2,1,0:T(8,128)S(1)}, u32[]{:S(2)}, u32[]{:S(2)}) collective-permute-start(f32[2,64,16,128]{3,2,1,0:T(8,128)} %get-tuple-element.24), channel_id=1, source_target_pairs={{4,0},{8,4},{12,8},{16,12},{20,16},{24,20},{28,24},{5,1},{9,5},{13... | collective-permute-start | bytes 3145736 | tf_op jit(solution)/shard_map/ppermute | solution.py:182
  92.6 4.0 %all-to-all-start.1 = ((f32[8,72,128]{2,1,0:T(8,128)}), f32[8,72,128]{2,1,0:T(8,128)}, u32[]{:S(2)}, u32[]{:S(2)}) async-start(f32[8,72,128]{2,1,0:T(8,128)} %get-tuple-element.17), calls=%async_computation.1 | async-start | bytes 589824 | tf_op jit(solution)/shard_map/all_to_all | solution.py:277
  96.8 7.4 %collective-permute-done.4.before_ref = f32[2,64,16,128]{3,2,1,0:T(8,128)S(1)} collective-permute-done((f32[2,64,16,128]{3,2,1,0:T(8,128)}, f32[2,64,16,128]{3,2,1,0:T(8,128)S(1)}, u32[]{:S(2)}, u32[]{:S(2)}) %collective-permute-start.4) | collective-permute-done | bytes 1048608 | tf_op jit(solution)/shard_map/ppermute | solution.py:182
  104.3 11.3 %collective-permute-done.5.after_ref = f32[2,64,16,128]{3,2,1,0:T(8,128)S(1)} collective-permute-done((f32[2,64,16,128]{3,2,1,0:T(8,128)}, f32[2,64,16,128]{3,2,1,0:T(8,128)S(1)}, u32[]{:S(2)}, u32[]{:S(2)}) %collective-permute-start.5) | collective-permute-done | bytes 1048608 | tf_op jit(solution)/shard_map/ppermute | solution.py:182
  115.6 7.8 %along_lon.3 = (f32[64,64,256]{2,1,0:T(8,128)}, f32[64,8,128]{2,1,0:T(8,128)S(1)}, f32[64,8,128]{2,1,0:T(8,128)S(1)}) custom-call(f32[64]{0:T(128)S(1)} %get-tuple-element.28.rate_ref, f32[64]{0:T(128)S(1)} %sqrt.3.scale_ref, f32[2,64,64,128]{3,2,1,0:T(8,128)} %bitcast.61, f32[2,64,16,128]{3,2,1,0:T(8,128)S(1)} %collective-permute-done.4.before_ref, ...), custom_call_target="tpu_custom_call" | custom-call | tf_op jit(solution)/shard_map/along_lon/pallas_call | solution.py:195
  123.4 3.2 %collective-permute-start.6 = (f32[64,8,128]{2,1,0:T(8,128)S(1)}, f32[64,8,128]{2,1,0:T(8,128)S(1)}, u32[]{:S(2)}, u32[]{:S(2)}) collective-permute-start(f32[64,8,128]{2,1,0:T(8,128)S(1)} %get-tuple-element.15), channel_id=1, source_target_pairs={{0,1},{1,2},{2,3},{4,5},{5,6},{6,7},{8,9},{9,10},{10,11},{12,13},{... | collective-permute-start | bytes 786440 | tf_op jit(solution)/shard_map/ppermute | solution.py:182
  126.6 1.3 collective-permute-start.7
  127.9 0.8 slice_compare_fusion
  128.7 2.0 %fusion.3 = f32[1,1,8,128,128]{3,4,2,1,0:T(8,128)S(1)} fusion(f32[1,1,8,128,128]{3,4,2,1,0:T(8,128)S(1)} %copy.16, f32[8,72,128]{2,1,0:T(8,128)} %all-to-all-done.1, f32[128]{0:T(128)S(1)} %copy-done.8, pred[8,128]{1,0:T(8,128)(4,1)S(1)} %bitcast.64, f32[128,64]{0,1:T(8,128)S(1)} %fusion.20), kind=kOutput, calls=%fused_computation.4 | convolution fusion | flops 101056512 | bytes 1345024 | tf_op jit(solution)/shard_map/cm,smk->sck/dot_general | solution.py:280
  130.7 1.0 copy.18
  131.7 2.0 %collective-permute-done.7.after_ref = f32[64,8,128]{2,1,0:T(8,128)S(1)} collective-permute-done((f32[64,8,128]{2,1,0:T(8,128)S(1)}, f32[64,8,128]{2,1,0:T(8,128)S(1)}, u32[]{:S(2)}, u32[]{:S(2)}) %collective-permute-start.7) | collective-permute-done | bytes 262176 | tf_op jit(solution)/shard_map/ppermute | solution.py:182
  133.8 2.2 %copy-done.3 = f32[64,64,256]{2,1,0:T(8,128)S(1)} copy-done((f32[64,64,256]{2,1,0:T(8,128)S(1)}, f32[64,64,256]{2,1,0:T(8,128)}, u32[]{:S(2)}) %copy-start.3) | copy-done | bytes 4194328
  135.9 9.0 %along_lat.3 = f32[64,64,256]{2,1,0:T(8,128)} custom-call(f32[64]{0:T(128)S(1)} %get-tuple-element.28.rate_ref, f32[64]{0:T(128)S(1)} %sqrt.3.scale_ref, f32[64,64,256]{2,1,0:T(8,128)S(1)} %copy-done.3, f32[64,8,128]{2,1,0:T(8,128)S(1)} %collective-permute-done.6.before_ref, f32[64,8,128]{2,1,0:T(8,128)S(1)} %collective-permute-done.7.after_ref, ...), custom_call_target="tpu_custom_call" | custom-call | tf_op jit(solution)/shard_map/along_lat/pallas_call | solution.py:220
  (29 shorter events, 0.6 us)
Async XLA Ops:
  0.6 9.8 %copy-start = (f32[128,127]{1,0:T(8,128)S(1)}, f32[128,127]{1,0:T(8,128)}, u32[]{:S(2)}) copy-start(f32[128,127]{1,0:T(8,128)} %param.11) | copy-start | bytes 195076
  0.6 9.8 %copy-start.7 = (f32[127,64]{0,1:T(8,128)S(1)}, f32[127,64]{0,1:T(8,128)}, u32[]{:S(2)}) copy-start(f32[127,64]{0,1:T(8,128)} %param.10) | copy-start | bytes 97540
  0.7 10.0 %copy-start.8 = (f32[128]{0:T(128)S(1)}, f32[128]{0:T(128)}, u32[]{:S(2)}) copy-start(f32[128]{0:T(128)} %param.12) | copy-start | bytes 1540
  0.7 10.0 %copy-start.6 = (f32[1,1,8,128,128]{4,3,2,1,0:T(8,128)S(1)}, f32[1,1,8,128,128]{4,3,2,1,0:T(8,128)}, u32[]{:S(2)}) copy-start(f32[1,1,8,128,128]{4,3,2,1,0:T(8,128)} %param.13) | copy-start | bytes 1572868
  0.7 15.5 %copy-start.9 = (f32[64]{0:T(128)S(1)}, f32[64]{0:T(128)}, u32[]{:S(2)}) copy-start(f32[64]{0:T(128)} %param.9) | copy-start | bytes 772
  3.8 43.5 %copy-start.4 = (s32[1,1,8,128]{3,2,1,0:T(8,128)S(1)}, s32[1,1,8,128]{3,2,1,0:T(8,128)}, u32[]{:S(2)}) copy-start(s32[1,1,8,128]{3,2,1,0:T(8,128)} %param.14) | copy-start | bytes 12292
  3.8 18.1 %collective-permute-start = (f32[64,16,256]{2,1,0:T(8,128)}, f32[64,16,256]{2,1,0:T(8,128)S(1)}, u32[]{:S(2)}, u32[]{:S(2)}) collective-permute-start(f32[64,16,256]{2,1,0:T(8,128)} %get-tuple-element.27), channel_id=1, source_target_pairs={{0,4},{4,8},{8,12},{12,16},{16,20},{20,24},{24,28},{1,5},{5,9},{9,... | collective-permute-start | bytes 3145736 | tf_op jit(solution)/shard_map/ppermute | solution.py:182
  8.5 26.5 %collective-permute-start.1 = (f32[64,16,256]{2,1,0:T(8,128)}, f32[64,16,256]{2,1,0:T(8,128)S(1)}, u32[]{:S(2)}, u32[]{:S(2)}) collective-permute-start(f32[64,16,256]{2,1,0:T(8,128)} %get-tuple-element.26), channel_id=1, source_target_pairs={{4,0},{8,4},{12,8},{16,12},{20,16},{24,20},{28,24},{5,1},{9,5},{13... | collective-permute-start | bytes 3145736 | tf_op jit(solution)/shard_map/ppermute | solution.py:182
  11.8 50.9 %all-to-all-start = ((f32[8,64,128]{2,1,0:T(8,128)}), f32[8,64,128]{2,1,0:T(8,128)S(1)}, u32[]{:S(2)}, u32[]{:S(2)}) async-start(f32[8,64,128]{2,1,0:T(8,128)} %convolution_bitcast_fusion.1), calls=%async_computation | async-start | bytes 524288 | tf_op jit(solution)/shard_map/all_to_all | solution.py:250
  42.8 6.5 %collective-permute-start.2 = (f32[64,8,128]{2,1,0:T(8,128)S(1)}, f32[64,8,128]{2,1,0:T(8,128)S(1)}, u32[]{:S(2)}, u32[]{:S(2)}) collective-permute-start(f32[64,8,128]{2,1,0:T(8,128)S(1)} %get-tuple-element.11), channel_id=1, source_target_pairs={{0,1},{1,2},{2,3},{4,5},{5,6},{6,7},{8,9},{9,10},{10,11},{12,13},{... | collective-permute-start | bytes 786440 | tf_op jit(solution)/shard_map/ppermute | solution.py:182
  46.0 7.1 %collective-permute-start.3 = (f32[64,8,128]{2,1,0:T(8,128)S(1)}, f32[64,8,128]{2,1,0:T(8,128)S(1)}, u32[]{:S(2)}, u32[]{:S(2)}) collective-permute-start(f32[64,8,128]{2,1,0:T(8,128)S(1)} %get-tuple-element.12), channel_id=1, source_target_pairs={{1,0},{2,1},{3,2},{5,4},{6,5},{7,6},{9,8},{10,9},{11,10},{13,12},{... | collective-permute-start | bytes 786440 | tf_op jit(solution)/shard_map/ppermute | solution.py:182
  53.1 9.6 %copy-start.5 = (s32[1,1,8]{2,1,0:T(1,128)S(1)}, s32[1,1,8]{2,1,0:T(1,128)}, u32[]{:S(2)}) copy-start(s32[1,1,8]{2,1,0:T(1,128)} %param.15) | copy-start | bytes 100
  60.7 2.0 %copy-start.1 = (f32[2,4096,128]{2,1,0:T(8,128)}, f32[2,4096,128]{2,1,0:T(8,128)S(1)}, u32[]{:S(2)}) copy-start(f32[2,4096,128]{2,1,0:T(8,128)S(1)} %along_lat.2.field_ref) | copy-start | bytes 12582916
  81.7 2.0 %copy-start.2 = (f32[2,4096,128]{2,1,0:T(8,128)}, f32[2,4096,128]{2,1,0:T(8,128)S(1)}, u32[]{:S(2)}) copy-start(f32[2,4096,128]{2,1,0:T(8,128)S(1)} %get-tuple-element.13) | copy-start | bytes 12582916
  85.2 19.1 %collective-permute-start.4 = (f32[2,64,16,128]{3,2,1,0:T(8,128)}, f32[2,64,16,128]{3,2,1,0:T(8,128)S(1)}, u32[]{:S(2)}, u32[]{:S(2)}) collective-permute-start(f32[2,64,16,128]{3,2,1,0:T(8,128)} %get-tuple-element.25), channel_id=1, source_target_pairs={{0,4},{4,8},{8,12},{12,16},{16,20},{20,24},{24,28},{1,5},{5,9},{9,... | collective-permute-start | bytes 3145736 | tf_op jit(solution)/shard_map/ppermute | solution.py:182
  90.7 25.0 %collective-permute-start.5 = (f32[2,64,16,128]{3,2,1,0:T(8,128)}, f32[2,64,16,128]{3,2,1,0:T(8,128)S(1)}, u32[]{:S(2)}, u32[]{:S(2)}) collective-permute-start(f32[2,64,16,128]{3,2,1,0:T(8,128)} %get-tuple-element.24), channel_id=1, source_target_pairs={{4,0},{8,4},{12,8},{16,12},{20,16},{24,20},{28,24},{5,1},{9,5},{13... | collective-permute-start | bytes 3145736 | tf_op jit(solution)/shard_map/ppermute | solution.py:182
  92.6 35.4 %all-to-all-start.1 = ((f32[8,72,128]{2,1,0:T(8,128)}), f32[8,72,128]{2,1,0:T(8,128)}, u32[]{:S(2)}, u32[]{:S(2)}) async-start(f32[8,72,128]{2,1,0:T(8,128)} %get-tuple-element.17), calls=%async_computation.1 | async-start | bytes 589824 | tf_op jit(solution)/shard_map/all_to_all | solution.py:277
  123.4 8.3 %collective-permute-start.6 = (f32[64,8,128]{2,1,0:T(8,128)S(1)}, f32[64,8,128]{2,1,0:T(8,128)S(1)}, u32[]{:S(2)}, u32[]{:S(2)}) collective-permute-start(f32[64,8,128]{2,1,0:T(8,128)S(1)} %get-tuple-element.15), channel_id=1, source_target_pairs={{0,1},{1,2},{2,3},{4,5},{5,6},{6,7},{8,9},{9,10},{10,11},{12,13},{... | collective-permute-start | bytes 786440 | tf_op jit(solution)/shard_map/ppermute | solution.py:182
  126.6 7.1 %collective-permute-start.7 = (f32[64,8,128]{2,1,0:T(8,128)S(1)}, f32[64,8,128]{2,1,0:T(8,128)S(1)}, u32[]{:S(2)}, u32[]{:S(2)}) collective-permute-start(f32[64,8,128]{2,1,0:T(8,128)S(1)} %get-tuple-element.16), channel_id=1, source_target_pairs={{1,0},{2,1},{3,2},{5,4},{6,5},{7,6},{9,8},{10,9},{11,10},{13,12},{... | collective-permute-start | bytes 786440 | tf_op jit(solution)/shard_map/ppermute | solution.py:182
  133.7 2.2 %copy-start.3 = (f32[64,64,256]{2,1,0:T(8,128)S(1)}, f32[64,64,256]{2,1,0:T(8,128)}, u32[]{:S(2)}) copy-start(f32[64,64,256]{2,1,0:T(8,128)} %get-tuple-element.14.y_ref) | copy-start | bytes 12582916
where the time goes:
time: 146 us; the launch traced here: 145 us
  Pallas kernels  51.2 us (35%)
  waiting for transfers between devices  45.1 us (31%)
  starting transfers between devices  31.3 us (21%)
  local copies, waits for them, and re-layouts  12.1 us (8%)
  matrix products  3.55 us (2%)
    ppermute x8, waiting for transfers between devices, from_neighbours(): return (lax.ppermute(last, axis, up), lax.ppermute(first, axis, down))  45.1 us
    ppermute x8, starting transfers between devices, from_neighbours(): return (lax.ppermute(last, axis, up), lax.ppermute(first, axis, down))  22.9 us
    pallas_call x1, Pallas kernels, shards(): pl.pallas_call(functools.partial(observe_kernel, lon), in_specs=[SMEM, SM...  18.9 us
    pallas_call x2, Pallas kernels, along_lat(): pl.pallas_call(functools.partial(lat_kernel, added is not None), grid=(mo...  16.6 us
    pallas_call x2, Pallas kernels, along_lon(): pl.pallas_call(functools.partial(lon_kernel, halves), grid=(modes // STEP...  15.6 us
    unnamed x23, local copies, waits for them, and re-layouts  7.44 us
    slice x2, local copies, waits for them, and re-layouts, along_lon(): lax.slice_in_dim(x, 0, REACH, axis=dim)  4.63 us
    all_to_all x1, starting transfers between devices, shards(): lax.all_to_all(projected, 'wide', split_axis=0, concat_axis=0, tiled=True)  4.36 us
  transfers between devices with their start and end apart: 10, of which 7 were waited for; matrix products, arithmetic and copies ran while one was open for 4% of the time, Pallas kernels for 16%

commit v1 on v0

v1 whole, which is shorter than its diff:
```python
import functools

import jax
import jax.numpy as jnp
from jax import lax
from jax.experimental import pallas as pl
from jax.experimental.pallas import tpu as pltpu
from jax.sharding import PartitionSpec as P

HALO = 15
REACH = 16
LANES = 128
STEP = 8
LAG = 2
HIGHEST = lax.Precision.HIGHEST
VMEM_BYTES = 48 * 2**20


def split(x):
    high = x.astype(jnp.bfloat16)
    return high, (x - high.astype(jnp.float32)).astype(jnp.bfloat16)


def taps(offset, rate, scale):
    curve = jnp.exp((offset * offset).astype(jnp.float32) * rate) * scale
    return jnp.where(jnp.abs(offset) <= HALO, curve, 0.0)


def lon_filter(halves, mode, rate_ref, scale_ref, x_ref, before_ref, after_ref, y_ref, first_ref, last_ref):
    lon = y_ref.shape[1]
    depth = lon + 2 * REACH
    row = lax.broadcasted_iota(jnp.int32, (lon, depth), 0)
    col = lax.broadcasted_iota(jnp.int32, (lon, depth), 1)
    offset = col - REACH - row
    lane = lax.broadcasted_iota(jnp.int32, (8, LANES), 1)
    if halves:
        x, before, after = (
            jnp.concatenate([ref[0, mode], ref[1, mode]], axis=1)
            for ref in (x_ref, before_ref, after_ref)
        )
    else:
        x, before, after = x_ref[mode], before_ref[mode], after_ref[mode]
    high, low = split(jnp.concatenate([before, x, after], axis=0))
    w_high, w_low = split(taps(offset, rate_ref[mode], scale_ref[mode]))
    both = jnp.dot(
        jnp.concatenate([w_high, w_low], axis=0), high, preferred_element_type=jnp.float32
    )
    y = both[:lon] + both[lon:]
    y = y + jnp.dot(w_high, low, preferred_element_type=jnp.float32)
    y_ref[mode] = y
    width = y.shape[1]
    first = jnp.zeros((8, LANES), jnp.float32)
    last = jnp.zeros((8, LANES), jnp.float32)
    for g in range(lon // 8):
        here = lane // REACH == g
        start = y[8 * g : 8 * g + 8, :LANES]
        end = y[8 * g : 8 * g + 8, width - LANES :]
        if g:
            start = pltpu.roll(start, REACH * g, 1)
        if g < 7:
            end = pltpu.roll(end, REACH * g + REACH, 1)
        first = jnp.where(here, start, first)
        last = jnp.where(here, end, last)
    first_ref[mode] = first
    last_ref[mode] = last


def lat_filter(mode, rate_ref, scale_ref, y_ref, before_ref, after_ref, added_ref, out_ref):
    lon, lat = y_ref.shape[1], y_ref.shape[2]
    tiles = lat // LANES
    depth = 2 * LANES
    row = lax.broadcasted_iota(jnp.int32, (depth, LANES), 0)
    col = lax.broadcasted_iota(jnp.int32, (depth, LANES), 1)
    offset = jnp.where(row < 3 * LANES // 2, row, row - depth) - col
    near = lax.broadcasted_iota(jnp.int32, (lon, LANES), 1) < LANES // 2
    before, after = before_ref[mode], after_ref[mode]
    lefts, rights = [], []
    for g in range(lon // 8):
        lefts.append(pltpu.roll(before, LANES - REACH - REACH * g, 1) if g < 7 else before)
        rights.append(pltpu.roll(after, LANES - REACH * g, 1) if g else after)
    blocks = [y_ref[mode, :, LANES * t : LANES * t + LANES] for t in range(tiles)]
    around = [jnp.concatenate(lefts, axis=0)] + blocks + [jnp.concatenate(rights, axis=0)]
    sides = [jnp.where(near, around[t + 2], around[t]) for t in range(tiles)]
    field = jnp.concatenate(
        [jnp.concatenate([blocks[t], sides[t]], axis=1) for t in range(tiles)], axis=0
    )
    high, low = split(field)
    w_high, w_low = split(taps(offset, rate_ref[mode], scale_ref[mode]))
    both = jnp.dot(
        jnp.concatenate([high, low], axis=0),
        jnp.concatenate([w_high, w_low], axis=1),
        preferred_element_type=jnp.float32,
    )
    count = tiles * lon
    z = both[:count, :LANES] + both[:count, LANES:] + both[count:, :LANES]
    for t in range(tiles):
        part = z[lon * t : lon * t + lon]
        if added_ref is not None:
            at = slice(LANES * t, LANES * t + LANES)
            out_ref[mode, :, at] = added_ref[mode, :, at] + part
        else:
            out_ref[t, mode] = part


def smooth_kernel(halves, add, rate_ref, scale_ref, x_ref, *rest):
    added_ref = rest[0] if add else None
    out_ref, y_ref, before_lon, after_lon, first_lat, last_lat, before_lat, after_lat = rest[add : add + 8]
    send_sems, recv_sems = rest[add + 8 :]
    modes, lon = y_ref.shape[0], y_ref.shape[1]
    chunks = modes // STEP
    axes = ("wide", "narrow")
    spot = [lax.axis_index(axis) for axis in axes]
    size = [lax.axis_size(axis) for axis in axes]
    exists = [spot[0] > 0, spot[0] < size[0] - 1, spot[1] > 0, spot[1] < size[1] - 1]
    target = [{axes[n // 2]: spot[n // 2] + (1 if n % 2 else -1)} for n in range(4)]

    def copy(n, c):
        at = pl.ds(c * STEP, STEP)
        if n < 2:
            rows = pl.ds(lon - REACH, REACH) if n else pl.ds(0, REACH)
            landing = before_lon if n else after_lon
            src = x_ref.at[:, at, rows] if halves else x_ref.at[at, rows]
            dst = landing.at[:, at] if halves else landing.at[at]
        else:
            src = (last_lat if n == 3 else first_lat).at[at]
            dst = (before_lat if n == 3 else after_lat).at[at]
        return pltpu.make_async_remote_copy(
            src_ref=src,
            dst_ref=dst,
            send_sem=send_sems.at[n, c],
            recv_sem=recv_sems.at[n, c],
            device_id=target[n],
            device_id_type=pl.DeviceIdType.MESH,
        )

    barrier = pltpu.get_barrier_semaphore()
    for n in range(4):
        @pl.when(exists[n])
        def _():
            pl.semaphore_signal(
                barrier, inc=1, device_id=target[n], device_id_type=pl.DeviceIdType.MESH
            )
    pl.semaphore_wait(barrier, sum(there.astype(jnp.int32) for there in exists))

    for n in range(2):
        @pl.when(exists[n])
        def _():
            @pl.loop(0, chunks)
            def _(c):
                copy(n, c).start()

    for n, landing in ((1, before_lon), (0, after_lon), (3, before_lat), (2, after_lat)):
        @pl.when(jnp.logical_not(exists[n ^ 1]))
        def _():
            landing[...] = jnp.zeros_like(landing)

    @pl.loop(0, chunks + LAG)
    def _(c):
        @pl.when(c < chunks)
        def _():
            for n in range(2):
                @pl.when(exists[n ^ 1])
                def _():
                    copy(n, c).wait_recv()
            for m in range(STEP):
                lon_filter(
                    halves, c * STEP + m, rate_ref, scale_ref, x_ref, before_lon, after_lon,
                    y_ref, first_lat, last_lat,
                )
            for n in range(2, 4):
                @pl.when(exists[n])
                def _():
                    copy(n, c).start()

        @pl.when(c >= LAG)
        def _():
            done = c - LAG
            for n in range(2, 4):
                @pl.when(exists[n ^ 1])
                def _():
                    copy(n, done).wait_recv()
            for m in range(STEP):
                lat_filter(
                    done * STEP + m, rate_ref, scale_ref, y_ref, before_lat, after_lat, added_ref, out_ref
                )

    for n in range(4):
        @pl.when(exists[n])
        def _():
            @pl.loop(0, chunks)
            def _(c):
                copy(n, c).wait_send()


def observe_kernel(lon, rows_ref, counts_ref, cols_ref, field_ref, normal_ref, offset_ref,
                   picked_ref, collected_ref, table, values):
    modes = normal_ref.shape[0]
    owners, slots = cols_ref.shape

    def to_table(i, carry):
        slab = jnp.concatenate(
            [field_ref[0, pl.ds(i, modes, stride=lon), :], field_ref[1, pl.ds(i, modes, stride=lon), :]],
            axis=0,
        )
        table[pl.ds(pl.multiple_of(i * LANES, LANES), LANES), :] = slab.T
        return carry

    lax.fori_loop(0, lon, to_table, 0, unroll=2)

    def pick(n, carry):
        for u in range(16):
            s = n * 16 + u
            values[pl.ds(s, 1), :] = table[pl.ds(rows_ref[s], 1), :]
        return carry

    lax.fori_loop(0, owners * slots // 16, pick, 0)
    table[...] = jnp.zeros_like(table)
    slot = lax.broadcasted_iota(jnp.int32, (modes, slots), 1)

    def respond(o, carry):
        at = pl.ds(pl.multiple_of(o * slots, slots), slots)
        both = values[at, :].T
        upper = (cols_ref[pl.ds(o, 1), :] & LANES) != 0
        picked = jnp.where(upper, both[modes:], both[:modes])
        count = counts_ref[o]
        picked_ref[o, :modes] = picked
        picked_ref[o, modes:] = jnp.full((8, slots), count.astype(jnp.float32))
        adjoint = jnp.dot(
            normal_ref[...], picked, precision=HIGHEST, preferred_element_type=jnp.float32
        ) - offset_ref[o]
        adjoint = jnp.where(slot < count, adjoint, 0.0)
        values[at, :] = jnp.concatenate(
            [jnp.where(upper, 0.0, adjoint), jnp.where(upper, adjoint, 0.0)], axis=0
        ).T
        return carry

    lax.fori_loop(0, owners, respond, 0)

    def collect(n, carry):
        for u in range(16):
            s = n * 16 + u
            row = rows_ref[s]
            table[pl.ds(row, 1), :] = table[pl.ds(row, 1), :] + values[pl.ds(s, 1), :]
        return carry

    lax.fori_loop(0, owners * slots // 16, collect, 0)

    def from_table(i, carry):
        slab = table[pl.ds(pl.multiple_of(i * LANES, LANES), LANES), :].T
        collected_ref[0, pl.ds(i, modes, stride=lon), :] = slab[:modes]
        collected_ref[1, pl.ds(i, modes, stride=lon), :] = slab[modes:]
        return carry

    lax.fori_loop(0, lon, from_table, 0, unroll=2)


SMEM = pl.BlockSpec(memory_space=pltpu.SMEM)


WHOLE = pl.BlockSpec(memory_space=pltpu.VMEM)


def smooth(x, rate, scale, shape, added=None):
    modes, lon, lat = shape
    halves = x.ndim == 4
    add = added is not None
    landing = (lat // LANES, modes, REACH, LANES) if halves else (modes, REACH, lat)
    out_shape = shape if add else (lat // LANES, modes, lon, LANES)
    return pl.pallas_call(
        functools.partial(smooth_kernel, halves, add),
        in_specs=[SMEM, SMEM, WHOLE] + [WHOLE] * add,
        out_specs=WHOLE,
        out_shape=jax.ShapeDtypeStruct(out_shape, jnp.float32),
        scratch_shapes=[pltpu.VMEM(shape, jnp.float32)]
        + [pltpu.VMEM(landing, jnp.float32)] * 2
        + [pltpu.VMEM((modes, 8, LANES), jnp.float32)] * 4
        + [pltpu.SemaphoreType.DMA((4, modes // STEP))] * 2,
        compiler_params=pltpu.CompilerParams(
            vmem_limit_bytes=VMEM_BYTES, collective_id=int(add), has_side_effects=True
        ),
        name="smooth_add" if add else "smooth",
    )(rate, scale, x, *((added,) if add else ()))


def shards(control, length_scale, modes, jacobian, obs_weight, departures, send_cols, counts):
    owners = lax.axis_size("wide")
    shape = control.shape
    mode_count, lon, lat = shape
    channels = jacobian.shape[0]
    slots = send_cols.shape[-1]
    tiles = lat // LANES

    offsets = jnp.arange(-HALO, HALO + 1).astype(jnp.float32)
    total = jnp.sum(jnp.exp(-(offsets[None, :] ** 2) / length_scale[:, None] ** 2), axis=1)
    rate = -0.5 / (length_scale * length_scale)
    scale = 1.0 / jnp.sqrt(total)

    forward = jnp.dot(jacobian, modes, precision=HIGHEST)
    weighted = obs_weight[:, None] * forward
    normal = jnp.dot(forward.T, weighted, precision=HIGHEST)
    observed = departures.reshape(owners, channels, slots)
    projected = jnp.einsum("cm,sck->smk", weighted, observed, precision=HIGHEST)
    offset = lax.all_to_all(projected, "wide", split_axis=0, concat_axis=0, tiled=True)

    columns = send_cols.reshape(owners, slots)
    rows = ((columns // lat) * LANES + columns % LANES).reshape(-1)

    smoothed = smooth(control, rate, scale, shape).reshape(tiles, mode_count * lon, LANES)
    outgoing, collected = pl.pallas_call(
        functools.partial(observe_kernel, lon),
        in_specs=[SMEM, SMEM] + [WHOLE] * 4,
        out_specs=[WHOLE, WHOLE],
        out_shape=[
            jax.ShapeDtypeStruct((owners, mode_count + 8, slots), jnp.float32),
            jax.ShapeDtypeStruct((tiles, mode_count * lon, LANES), jnp.float32),
        ],
        scratch_shapes=[
            pltpu.VMEM((lon * LANES, LANES), jnp.float32),
            pltpu.VMEM((owners * slots, LANES), jnp.float32),
        ],
        compiler_params=pltpu.CompilerParams(vmem_limit_bytes=VMEM_BYTES),
        name="observe",
    )(rows, counts.reshape(owners), columns, smoothed, normal, offset)

    arrived = lax.all_to_all(outgoing, "wide", split_axis=0, concat_axis=0, tiled=True)
    gradient = smooth(
        collected.reshape(tiles, mode_count, lon, LANES), rate, scale, shape, control
    )

    evolved = jnp.einsum("cm,smk->sck", forward, arrived[:, :mode_count], precision=HIGHEST)
    live = jnp.arange(slots).astype(jnp.float32) < arrived[:, mode_count, :]
    residual = jnp.where(
        live[:, None, :], obs_weight[None, :, None] * (evolved - observed), jnp.float32(0.0)
    )
    return (gradient, residual.reshape(departures.shape))


def solution(mesh):
    in_specs = (
        P(None, "wide", "narrow"),
        P(),
        P(),
        P(),
        P(),
        P("wide", "narrow", None, None, None),
        P("wide", "narrow", None, None),
        P("wide", "narrow", None),
    )
    out_specs = (P(None, "wide", "narrow"), P("wide", "narrow", None, None, None))
    return jax.shard_map(shards, mesh=mesh, in_specs=in_specs, out_specs=out_specs, check_vma=False)
```

time: 146 us -> 115 us (0.79)
  waiting for transfers between devices: 45.1 us -> 0.01 us
  Pallas kernels: 51.2 us -> 86.2 us
  starting transfers between devices: 31.3 us -> 8.86 us
    ppermute x8 -> x0, waiting for transfers between devices: 45.1 us -> none  [from_neighbours(): return (lax.ppermute(last, axis, up), lax.ppermute(first, axis, down))]
    pallas_call x4 -> x2, Pallas kernels: 32.2 us -> 67.3 us  [smooth(): pl.pallas_call(functools.partial(smooth_kernel, halves, add), in_specs=[S...]
    ppermute x8 -> x0, starting transfers between devices: 22.9 us -> none  [from_neighbours(): return (lax.ppermute(last, axis, up), lax.ppermute(first, axis, down))]
    unnamed x23 -> x20, local copies, waits for them, and re-layouts: 7.44 us -> 12.7 us
    slice x2 -> x0, local copies, waits for them, and re-layouts: 4.63 us -> none  [along_lon(): lax.slice_in_dim(x, 0, REACH, axis=dim)]
  transfers between devices with their start and end apart: 10 -> 2, of which waited for: 7 -> 0; matrix products, arithmetic and copies ran while one was open for 4% -> 2% of each run, Pallas kernels for 16% -> 59%
where the time goes in v1:
time: 115 us; the launch traced here: 114 us
  Pallas kernels  86.2 us (75%)
  local copies, waits for them, and re-layouts  12.7 us (11%)
  starting transfers between devices  8.86 us (8%)
  matrix products  4.41 us (4%)
  other arithmetic  1.47 us (1%)
    pallas_call x2, Pallas kernels, smooth(): pl.pallas_call(functools.partial(smooth_kernel, halves, add), in_specs=[S...  67.3 us
    pallas_call x1, Pallas kernels, shards(): pl.pallas_call(functools.partial(observe_kernel, lon), in_specs=[SMEM, SM...  18.9 us
    unnamed x20, local copies, waits for them, and re-layouts  12.7 us
    all_to_all x1, starting transfers between devices, shards(): lax.all_to_all(projected, 'wide', split_axis=0, concat_axis=0, tiled=True)  5.22 us
    all_to_all x1, starting transfers between devices, shards(): lax.all_to_all(outgoing, 'wide', split_axis=0, concat_axis=0, tiled=True)  3.64 us
  transfers between devices with their start and end apart: 2, of which 0 were waited for; matrix products, arithmetic and copies ran while one was open for 2% of the time, Pallas kernels for 59%

profile of v1, /device:TPU:1, one launch (start us, length us, event | category | flops | bytes accessed | tf_op | source)
XLA Modules:
  0.0 114.5 jit_solution(2467996503244136109)
XLA Ops:
  0.6 0.0 copy-start
  0.6 0.8 copy-done
  1.5 1.0 fusion.18
  2.5 2.2 %convolution_bitcast_fusion.1 = f32[8,64,128]{2,1,0:T(8,128)} fusion(f32[1,1,8,128,128]{4,3,2,1,0:T(8,128)} %param.13, f32[128,64]{0,1:T(8,128)S(1)} %fusion.18, f32[128]{0:T(128)} %param.12), kind=kOutput, calls=%fused_computation.5 | convolution fusion | flops 100671488 | bytes 819712 | tf_op jit(solution)/shard_map/cm,sck->smk/dot_general | solution.py:302
  4.7 5.2 %all-to-all-start = ((f32[8,64,128]{2,1,0:T(8,128)}), f32[8,64,128]{2,1,0:T(8,128)S(1)}, u32[]{:S(2)}, u32[]{:S(2)}) async-start(f32[8,64,128]{2,1,0:T(8,128)} %convolution_bitcast_fusion.1), calls=%async_computation | async-start | bytes 524288 | tf_op jit(solution)/shard_map/all_to_all | solution.py:303
  9.9 0.7 broadcast_divide_fusion
  10.6 0.7 fusion.14.rows_ref
  11.3 0.1 fusion.9
  11.4 0.0 copy-start.7
  11.4 0.0 copy-start.4
  11.4 0.0 copy-start.5
  11.4 32.9 %smooth.1 = f32[2,64,64,128]{3,2,1,0:T(8,128)S(1)} custom-call(f32[64]{0:T(128)S(1)} %get-tuple-element.12.rate_ref, f32[64]{0:T(128)S(1)} %sqrt.3.scale_ref, f32[64,64,256]{2,1,0:T(8,128)} %rest_0_.1), custom_call_target="tpu_custom_call" | custom-call | tf_op jit(solution)/shard_map/smooth/pallas_call | solution.py:269
  44.3 0.0 copy-start.2
  44.3 2.0 %copy-done.2 = f32[2,64,64,128]{3,2,1,0:T(8,128)} copy-done((f32[2,64,64,128]{3,2,1,0:T(8,128)}, f32[2,64,64,128]{3,2,1,0:T(8,128)S(1)}, u32[]{:S(2)}) %copy-start.2) | copy-done | bytes 4194328
  46.3 0.0 copy-done.7
  46.3 0.2 fusion.6.normal_ref
  46.5 0.0 all-to-all-done.offset_ref
  46.5 0.0 copy-done.4
  46.5 0.0 copy-done.5
  46.5 18.9 %observe.1 = (f32[8,72,128]{2,1,0:T(8,128)}, f32[2,4096,128]{2,1,0:T(8,128)S(1)}) custom-call(s32[1024]{0:T(1024)S(1)} %fusion.14.rows_ref, s32[8]{0:T(128)S(1)} %bitcast.64, s32[8,128]{1,0:T(8,128)S(1)} %bitcast.63, f32[2,4096,128]{2,1,0:T(8,128)} %bitcast.61, f32[64,64]{1,0:T(8,128)S(1)} %fusion.6.normal_ref, f32[8,64,128]{2,1,0:T(8,128)S(1)} %all-to-all-done.offset_ref), custom_call_target="tpu_custom_call" | custom-call | tf_op jit(solution)/shard_map/observe/pallas_call | solution.py:309
  65.5 0.0 copy-start.3
  65.5 2.0 %copy-done.3 = f32[2,4096,128]{2,1,0:T(8,128)} copy-done((f32[2,4096,128]{2,1,0:T(8,128)}, f32[2,4096,128]{2,1,0:T(8,128)S(1)}, u32[]{:S(2)}) %copy-start.3) | copy-done | bytes 4194328
  67.5 3.6 %all-to-all-start.1 = ((f32[8,72,128]{2,1,0:T(8,128)}), f32[8,72,128]{2,1,0:T(8,128)S(1)}, u32[]{:S(2)}, u32[]{:S(2)}) async-start(f32[8,72,128]{2,1,0:T(8,128)} %get-tuple-element.5), calls=%async_computation.1 | async-start | bytes 589824 | tf_op jit(solution)/shard_map/all_to_all | solution.py:325
  71.1 0.0 copy-done.6
  71.1 0.2 copy.16
  71.3 34.4 %smooth_add.1 = f32[64,64,256]{2,1,0:T(8,128)S(1)} custom-call(f32[64]{0:T(128)S(1)} %get-tuple-element.12.rate_ref, f32[64]{0:T(128)S(1)} %sqrt.3.scale_ref, f32[2,64,64,128]{3,2,1,0:T(8,128)} %bitcast.62, f32[64,64,256]{2,1,0:T(8,128)} %rest_0_.1), custom_call_target="tpu_custom_call" | custom-call | tf_op jit(solution)/shard_map/smooth_add/pallas_call | solution.py:269
  105.7 0.0 copy-start.1
  105.8 1.9 %copy-done.1 = f32[64,64,256]{2,1,0:T(8,128)} copy-done((f32[64,64,256]{2,1,0:T(8,128)}, f32[64,64,256]{2,1,0:T(8,128)S(1)}, u32[]{:S(2)}) %copy-start.1) | copy-done | bytes 4194328
  107.7 0.0 all-to-all-done.1
  107.7 1.0 fusion.3
  108.8 1.0 copy.18
  109.8 4.7 %copy.26 = f32[64,64,256]{2,1,0:T(8,128)} copy(f32[64,64,256]{2,1,0:T(8,128)} %copy-done.1) | data formatting | bytes 8388608
  (6 shorter events, 0.0 us)
Async XLA Ops:
  0.6 0.8 copy-start
  4.7 41.8 %all-to-all-start = ((f32[8,64,128]{2,1,0:T(8,128)}), f32[8,64,128]{2,1,0:T(8,128)S(1)}, u32[]{:S(2)}, u32[]{:S(2)}) async-start(f32[8,64,128]{2,1,0:T(8,128)} %convolution_bitcast_fusion.1), calls=%async_computation | async-start | bytes 524288 | tf_op jit(solution)/shard_map/all_to_all | solution.py:303
  11.4 34.9 %copy-start.7 = (f32[128]{0:T(128)S(1)}, f32[128]{0:T(128)}, u32[]{:S(2)}) copy-start(f32[128]{0:T(128)} %param.12) | copy-start | bytes 1540
  11.4 35.1 %copy-start.4 = (s32[1,1,8,128]{3,2,1,0:T(8,128)S(1)}, s32[1,1,8,128]{3,2,1,0:T(8,128)}, u32[]{:S(2)}) copy-start(s32[1,1,8,128]{3,2,1,0:T(8,128)} %param.14) | copy-start | bytes 12292
  11.4 35.1 %copy-start.5 = (s32[1,1,8]{2,1,0:T(1,128)S(1)}, s32[1,1,8]{2,1,0:T(1,128)}, u32[]{:S(2)}) copy-start(s32[1,1,8]{2,1,0:T(1,128)} %param.15) | copy-start | bytes 100
  44.3 2.0 %copy-start.2 = (f32[2,64,64,128]{3,2,1,0:T(8,128)}, f32[2,64,64,128]{3,2,1,0:T(8,128)S(1)}, u32[]{:S(2)}) copy-start(f32[2,64,64,128]{3,2,1,0:T(8,128)S(1)} %smooth.1) | copy-start | bytes 12582916
  46.3 24.8 %copy-start.6 = (f32[1,1,8,128,128]{4,3,2,1,0:T(8,128)S(1)}, f32[1,1,8,128,128]{4,3,2,1,0:T(8,128)}, u32[]{:S(2)}) copy-start(f32[1,1,8,128,128]{4,3,2,1,0:T(8,128)} %param.13) | copy-start | bytes 1572868
  65.5 2.0 %copy-start.3 = (f32[2,4096,128]{2,1,0:T(8,128)}, f32[2,4096,128]{2,1,0:T(8,128)S(1)}, u32[]{:S(2)}) copy-start(f32[2,4096,128]{2,1,0:T(8,128)S(1)} %get-tuple-element.4) | copy-start | bytes 12582916
  67.5 40.2 %all-to-all-start.1 = ((f32[8,72,128]{2,1,0:T(8,128)}), f32[8,72,128]{2,1,0:T(8,128)S(1)}, u32[]{:S(2)}, u32[]{:S(2)}) async-start(f32[8,72,128]{2,1,0:T(8,128)} %get-tuple-element.5), calls=%async_computation.1 | async-start | bytes 589824 | tf_op jit(solution)/shard_map/all_to_all | solution.py:325
  105.7 2.0 %copy-start.1 = (f32[64,64,256]{2,1,0:T(8,128)}, f32[64,64,256]{2,1,0:T(8,128)S(1)}, u32[]{:S(2)}) copy-start(f32[64,64,256]{2,1,0:T(8,128)S(1)} %smooth_add.1) | copy-start | bytes 12582916

commit v2 on v1

--- a/solution.py
+++ b/solution.py
@@ -13,7 +13,7 @@
 STEP = 8
 LAG = 2
 HIGHEST = lax.Precision.HIGHEST
-VMEM_BYTES = 48 * 2**20
+VMEM_BYTES = 24 * 2**20
 
 
 def split(x):
@@ -65,7 +65,7 @@
     last_ref[mode] = last
 
 
-def lat_filter(mode, rate_ref, scale_ref, y_ref, before_ref, after_ref, added_ref, out_ref):
+def lat_filter(mode, rate_ref, scale_ref, y_ref, before_ref, after_ref, out_ref):
     lon, lat = y_ref.shape[1], y_ref.shape[2]
     tiles = lat // LANES
     depth = 2 * LANES
@@ -95,17 +95,15 @@
     z = both[:count, :LANES] + both[:count, LANES:] + both[count:, :LANES]
     for t in range(tiles):
         part = z[lon * t : lon * t + lon]
-        if added_ref is not None:
-            at = slice(LANES * t, LANES * t + LANES)
-            out_ref[mode, :, at] = added_ref[mode, :, at] + part
+        if len(out_ref.shape) == 3:
+            out_ref[mode, :, LANES * t : LANES * t + LANES] = part
         else:
             out_ref[t, mode] = part
 
 
-def smooth_kernel(halves, add, rate_ref, scale_ref, x_ref, *rest):
-    added_ref = rest[0] if add else None
-    out_ref, y_ref, before_lon, after_lon, first_lat, last_lat, before_lat, after_lat = rest[add : add + 8]
-    send_sems, recv_sems = rest[add + 8 :]
+def smooth_kernel(halves, rate_ref, scale_ref, x_ref, parcel_ref, out_ref, arrived_ref, y_ref,
+                  before_lon, after_lon, first_lat, last_lat, before_lat, after_lat,
+                  send_sems, recv_sems, parcel_send, parcel_recv):
     modes, lon = y_ref.shape[0], y_ref.shape[1]
     chunks = modes // STEP
     axes = ("wide", "narrow")
@@ -133,14 +131,32 @@
             device_id_type=pl.DeviceIdType.MESH,
         )
 
+    def parcel(p):
+        peer = lax.rem(spot[0] + p, size[0])
+        return pltpu.make_async_remote_copy(
+            src_ref=parcel_ref.at[peer],
+            dst_ref=arrived_ref.at[spot[0]],
+            send_sem=parcel_send.at[p],
+            recv_sem=parcel_recv.at[p],
+            device_id={"wide": peer},
+            device_id_type=pl.DeviceIdType.MESH,
+        )
+
     barrier = pltpu.get_barrier_semaphore()
-    for n in range(4):
+
+    @pl.loop(1, size[0])
+    def _(p):
+        pl.semaphore_signal(
+            barrier, inc=1, device_id={"wide": lax.rem(spot[0] + p, size[0])},
+            device_id_type=pl.DeviceIdType.MESH,
+        )
+    for n in range(2, 4):
         @pl.when(exists[n])
         def _():
             pl.semaphore_signal(
                 barrier, inc=1, device_id=target[n], device_id_type=pl.DeviceIdType.MESH
             )
-    pl.semaphore_wait(barrier, sum(there.astype(jnp.int32) for there in exists))
+    pl.semaphore_wait(barrier, size[0] - 1 + sum(there.astype(jnp.int32) for there in exists[2:]))
 
     for n in range(2):
         @pl.when(exists[n])
@@ -148,6 +164,12 @@
             @pl.loop(0, chunks)
             def _(c):
                 copy(n, c).start()
+
+    @pl.loop(1, size[0])
+    def _(p):
+        parcel(p).start()
+
+    arrived_ref[spot[0]] = parcel_ref[spot[0]]
 
     for n, landing in ((1, before_lon), (0, after_lon), (3, before_lat), (2, after_lat)):
         @pl.when(jnp.logical_not(exists[n ^ 1]))
@@ -181,7 +203,7 @@
                     copy(n, done).wait_recv()
             for m in range(STEP):
                 lat_filter(
-                    done * STEP + m, rate_ref, scale_ref, y_ref, before_lat, after_lat, added_ref, out_ref
+                    done * STEP + m, rate_ref, scale_ref, y_ref, before_lat, after_lat, out_ref
                 )
 
     for n in range(4):
@@ -190,6 +212,10 @@
             @pl.loop(0, chunks)
             def _(c):
                 copy(n, c).wait_send()
+
+    @pl.loop(1, size[0])
+    def _(p):
+        parcel(p).wait()
 
 
 def observe_kernel(lon, rows_ref, counts_ref, cols_ref, field_ref, normal_ref, offset_ref,
@@ -260,26 +286,29 @@
 WHOLE = pl.BlockSpec(memory_space=pltpu.VMEM)
 
 
-def smooth(x, rate, scale, shape, added=None):
+def smooth(x, parcel, rate, scale, shape):
     modes, lon, lat = shape
     halves = x.ndim == 4
-    add = added is not None
     landing = (lat // LANES, modes, REACH, LANES) if halves else (modes, REACH, lat)
-    out_shape = shape if add else (lat // LANES, modes, lon, LANES)
+    out_shape = shape if halves else (lat // LANES, modes, lon, LANES)
     return pl.pallas_call(
-        functools.partial(smooth_kernel, halves, add),
-        in_specs=[SMEM, SMEM, WHOLE] + [WHOLE] * add,
-        out_specs=WHOLE,
-        out_shape=jax.ShapeDtypeStruct(out_shape, jnp.float32),
+        functools.partial(smooth_kernel, halves),
+        in_specs=[SMEM, SMEM, WHOLE, WHOLE],
+        out_specs=[WHOLE, WHOLE],
+        out_shape=[
+            jax.ShapeDtypeStruct(out_shape, jnp.float32),
+            jax.ShapeDtypeStruct(parcel.shape, jnp.float32),
+        ],
         scratch_shapes=[pltpu.VMEM(shape, jnp.float32)]
         + [pltpu.VMEM(landing, jnp.float32)] * 2
         + [pltpu.VMEM((modes, 8, LANES), jnp.float32)] * 4
-        + [pltpu.SemaphoreType.DMA((4, modes // STEP))] * 2,
+        + [pltpu.SemaphoreType.DMA((4, modes // STEP))] * 2
+        + [pltpu.SemaphoreType.DMA((parcel.shape[0],))] * 2,
         compiler_params=pltpu.CompilerParams(
-            vmem_limit_bytes=VMEM_BYTES, collective_id=int(add), has_side_effects=True
+            vmem_limit_bytes=VMEM_BYTES, collective_id=int(halves), has_side_effects=True
         ),
-        name="smooth_add" if add else "smooth",
-    )(rate, scale, x, *((added,) if add else ()))
+        name="smooth_back" if halves else "smooth",
+    )(rate, scale, x, parcel)
 
 
 def shards(control, length_scale, modes, jacobian, obs_weight, departures, send_cols, counts):
@@ -300,12 +329,12 @@
     normal = jnp.dot(forward.T, weighted, precision=HIGHEST)
     observed = departures.reshape(owners, channels, slots)
     projected = jnp.einsum("cm,sck->smk", weighted, observed, precision=HIGHEST)
-    offset = lax.all_to_all(projected, "wide", split_axis=0, concat_axis=0, tiled=True)
 
     columns = send_cols.reshape(owners, slots)
     rows = ((columns // lat) * LANES + columns % LANES).reshape(-1)
 
-    smoothed = smooth(control, rate, scale, shape).reshape(tiles, mode_count * lon, LANES)
+    smoothed, offset = smooth(control, projected, rate, scale, shape)
+    smoothed = smoothed.reshape(tiles, mode_count * lon, LANES)
     outgoing, collected = pl.pallas_call(
         functools.partial(observe_kernel, lon),
         in_specs=[SMEM, SMEM] + [WHOLE] * 4,
@@ -322,10 +351,10 @@
         name="observe",
     )(rows, counts.reshape(owners), columns, smoothed, normal, offset)
 
-    arrived = lax.all_to_all(outgoing, "wide", split_axis=0, concat_axis=0, tiled=True)
-    gradient = smooth(
-        collected.reshape(tiles, mode_count, lon, LANES), rate, scale, shape, control
-    )
+    response, arrived = smooth(
+        collected.reshape(tiles, mode_count, lon, LANES), outgoing, rate, scale, shape
+    )
+    gradient = control + response
 
     evolved = jnp.einsum("cm,smk->sck", forward, arrived[:, :mode_count], precision=HIGHEST)
     live = jnp.arange(slots).astype(jnp.float32) < arrived[:, mode_count, :]

time: 115 us -> 100 us (0.87)
  starting transfers between devices: 8.86 us -> 0 us
  local copies, waits for them, and re-layouts: 12.7 us -> 6.24 us
  other arithmetic: 1.47 us -> 7.36 us
  Pallas kernels: 86.2 us -> 81.7 us
    all_to_all x2 -> x0, starting transfers between devices: 8.86 us -> none  [the longest x1 5.22 us: shards(): lax.all_to_all(projected, 'wide', split_axis=0, concat_axis=0, tiled=True)]
    add x0 -> x1, other arithmetic: none -> 6.56 us  [shards(): gradient = control + response]
    unnamed x20 -> x17, local copies, waits for them, and re-layouts: 12.7 us -> 6.23 us
    pallas_call x2, Pallas kernels: 67.3 us -> 65 us  [smooth(): pl.pallas_call(functools.partial(smooth_kernel, halves), in_specs=[SMEM,...]
    pallas_call x1, Pallas kernels: 18.9 us -> 16.7 us  [shards(): pl.pallas_call(functools.partial(observe_kernel, lon), in_specs=[SMEM, SM...]
  transfers between devices with their start and end apart: 2 -> 0, of which waited for: 0 -> 0; matrix products, arithmetic and copies ran while one was open for 2% -> 0% of each run, Pallas kernels for 59% -> 0%
where the time goes in v2:
time: 100 us; the launch traced here: 99.8 us
  Pallas kernels  81.7 us (82%)
  other arithmetic  7.36 us (7%)
  local copies, waits for them, and re-layouts  6.24 us (6%)
  matrix products  3.71 us (4%)
    pallas_call x2, Pallas kernels, smooth(): pl.pallas_call(functools.partial(smooth_kernel, halves), in_specs=[SMEM,...  65 us
    pallas_call x1, Pallas kernels, shards(): pl.pallas_call(functools.partial(observe_kernel, lon), in_specs=[SMEM, SM...  16.7 us
    add x1, other arithmetic, shards(): gradient = control + response  6.56 us
    unnamed x17, local copies, waits for them, and re-layouts  6.23 us

profile of v2, /device:TPU:1, one launch (start us, length us, event | category | flops | bytes accessed | tf_op | source)
XLA Modules:
  0.0 99.8 jit_solution(3230347076528063992)
XLA Ops:
  0.6 0.0 copy-start
  0.6 0.0 copy-start.6
  0.7 0.0 copy-start.3
  0.7 0.8 copy-done
  1.5 0.0 copy-start.4
  1.5 1.0 %fusion.18 = f32[128,64]{0,1:T(8,128)S(1)} fusion(f32[128,127]{1,0:T(8,128)S(1)} %copy-done, f32[127,64]{0,1:T(8,128)} %param.10), kind=kOutput, calls=%fused_computation.35 | convolution fusion | flops 12484608 | bytes 130304 | tf_op jit(solution)/shard_map/dot_general | solution.py:327
  2.5 1.5 %convolution_bitcast_fusion.1.parcel_ref = f32[8,64,128]{2,1,0:T(8,128)S(1)} fusion(f32[1,1,8,128,128]{4,3,2,1,0:T(8,128)} %param.13, f32[128,64]{0,1:T(8,128)S(1)} %fusion.18, f32[128]{0:T(128)} %param.12), kind=kOutput, calls=%fused_computation.5 | convolution fusion | flops 100671488 | bytes 819712 | tf_op jit(solution)/shard_map/cm,sck->smk/dot_general | solution.py:331
  4.0 0.7 broadcast_divide_fusion
  4.7 0.1 fusion.9
  4.8 0.0 copy-start.1
  4.8 2.2 %copy-done.1 = f32[64,64,256]{2,1,0:T(8,128)S(1)} copy-done((f32[64,64,256]{2,1,0:T(8,128)S(1)}, f32[64,64,256]{2,1,0:T(8,128)}, u32[]{:S(2)}) %copy-start.1) | copy-done | bytes 4194328
  7.0 33.1 %smooth.1 = (f32[2,64,64,128]{3,2,1,0:T(8,128)S(1)}, f32[8,64,128]{2,1,0:T(8,128)S(1)}) custom-call(f32[64]{0:T(128)S(1)} %get-tuple-element.20.rate_ref, f32[64]{0:T(128)S(1)} %sqrt.3.scale_ref, f32[64,64,256]{2,1,0:T(8,128)S(1)} %copy-done.1, f32[8,64,128]{2,1,0:T(8,128)S(1)} %convolution_bitcast_fusion.1.parcel_ref), custom_call_target="tpu_custom_call" | custom-call | tf_op jit(solution)/shard_map/smooth/pallas_call | solution.py:294
  40.1 0.0 copy-done.6
  40.1 0.2 fusion.6.normal_ref
  40.3 0.0 copy-done.3
  40.3 0.0 copy-done.4
  40.3 0.0 copy-start.5
  40.3 16.7 %observe.1 = (f32[8,72,128]{2,1,0:T(8,128)S(1)}, f32[2,4096,128]{2,1,0:T(8,128)S(1)}) custom-call(s32[1024]{0:T(1024)S(1)} %fusion.14.rows_ref, s32[8]{0:T(128)S(1)} %bitcast.64, s32[8,128]{1,0:T(8,128)S(1)} %bitcast.63, f32[2,4096,128]{2,1,0:T(8,128)S(1)} %bitcast.62, f32[64,64]{1,0:T(8,128)S(1)} %fusion.6.normal_ref, ...), custom_call_target="tpu_custom_call" | custom-call | tf_op jit(solution)/shard_map/observe/pallas_call | solution.py:338
  57.1 31.8 %smooth_back.1 = (f32[64,64,256]{2,1,0:T(8,128)S(1)}, f32[8,72,128]{2,1,0:T(8,128)S(1)}) custom-call(f32[64]{0:T(128)S(1)} %get-tuple-element.20.rate_ref, f32[64]{0:T(128)S(1)} %sqrt.3.scale_ref, f32[2,64,64,128]{3,2,1,0:T(8,128)S(1)} %bitcast.61, f32[8,72,128]{2,1,0:T(8,128)S(1)} %get-tuple-element.11.parcel_ref), custom_call_target="tpu_custom_call" | custom-call | tf_op jit(solution)/shard_map/smooth_back/pallas_call | solution.py:294
  88.9 0.0 copy-start.2
  88.9 2.0 %copy-done.2 = f32[64,64,256]{2,1,0:T(8,128)} copy-done((f32[64,64,256]{2,1,0:T(8,128)}, f32[64,64,256]{2,1,0:T(8,128)S(1)}, u32[]{:S(2)}) %copy-start.2) | copy-done | bytes 4194328
  91.0 0.0 copy-done.5
  91.0 0.2 copy.16
  91.2 1.0 %fusion.3 = f32[1,1,8,128,128]{3,4,2,1,0:T(8,128)S(1)} fusion(f32[1,1,8,128,128]{3,4,2,1,0:T(8,128)S(1)} %copy.16, f32[8,72,128]{2,1,0:T(8,128)S(1)} %get-tuple-element.13, f32[128]{0:T(128)S(1)} %copy-done.6, pred[8,128]{1,0:T(8,128)(4,1)S(1)} %bitcast.65, f32[128,64]{0,1:T(8,128)S(1)} %fusion.18), kind=kOutput, calls=%fused_computation.4 | convolution fusion | flops 101056512 | bytes 1345024 | tf_op jit(solution)/shard_map/cm,smk->sck/dot_general | solution.py:359
  92.2 1.0 copy.18
  93.2 6.6 %add.26 = f32[64,64,256]{2,1,0:T(8,128)} add(f32[64,64,256]{2,1,0:T(8,128)} %x_ref.1, f32[64,64,256]{2,1,0:T(8,128)} %copy-done.2) | non-fusion elementwise | flops 1048576 | bytes 12582912 | tf_op jit(solution)/shard_map/add | solution.py:357
  (6 shorter events, 0.0 us)
Async XLA Ops:
  0.6 0.8 copy-start
  0.6 39.4 %copy-start.6 = (f32[128]{0:T(128)S(1)}, f32[128]{0:T(128)}, u32[]{:S(2)}) copy-start(f32[128]{0:T(128)} %param.12) | copy-start | bytes 1540
  0.7 39.6 %copy-start.3 = (s32[1,1,8,128]{3,2,1,0:T(8,128)S(1)}, s32[1,1,8,128]{3,2,1,0:T(8,128)}, u32[]{:S(2)}) copy-start(s32[1,1,8,128]{3,2,1,0:T(8,128)} %param.14) | copy-start | bytes 12292
  1.5 38.8 %copy-start.4 = (s32[1,1,8]{2,1,0:T(1,128)S(1)}, s32[1,1,8]{2,1,0:T(1,128)}, u32[]{:S(2)}) copy-start(s32[1,1,8]{2,1,0:T(1,128)} %param.15) | copy-start | bytes 100
  4.8 2.2 %copy-start.1 = (f32[64,64,256]{2,1,0:T(8,128)S(1)}, f32[64,64,256]{2,1,0:T(8,128)}, u32[]{:S(2)}) copy-start(f32[64,64,256]{2,1,0:T(8,128)} %x_ref.1) | copy-start | bytes 12582916
  40.3 50.6 %copy-start.5 = (f32[1,1,8,128,128]{4,3,2,1,0:T(8,128)S(1)}, f32[1,1,8,128,128]{4,3,2,1,0:T(8,128)}, u32[]{:S(2)}) copy-start(f32[1,1,8,128,128]{4,3,2,1,0:T(8,128)} %param.13) | copy-start | bytes 1572868
  88.9 2.0 %copy-start.2 = (f32[64,64,256]{2,1,0:T(8,128)}, f32[64,64,256]{2,1,0:T(8,128)S(1)}, u32[]{:S(2)}) copy-start(f32[64,64,256]{2,1,0:T(8,128)S(1)} %get-tuple-element.12) | copy-start | bytes 12582916

commit v3 on v2

--- a/solution.py
+++ b/solution.py
@@ -311,6 +311,23 @@
     )(rate, scale, x, parcel)
 
 
+def add_kernel(a_ref, b_ref, out_ref):
+    out_ref[...] = a_ref[...] + b_ref[...]
+
+
+def plus(a, b):
+    block = pl.BlockSpec((STEP,) + a.shape[1:], lambda g: (g, 0, 0))
+    return pl.pallas_call(
+        add_kernel,
+        grid=(a.shape[0] // STEP,),
+        in_specs=[block, block],
+        out_specs=block,
+        out_shape=jax.ShapeDtypeStruct(a.shape, a.dtype),
+        compiler_params=pltpu.CompilerParams(vmem_limit_bytes=VMEM_BYTES),
+        name="plus",
+    )(a, b)
+
+
 def shards(control, length_scale, modes, jacobian, obs_weight, departures, send_cols, counts):
     owners = lax.axis_size("wide")
     shape = control.shape
@@ -354,7 +371,7 @@
     response, arrived = smooth(
         collected.reshape(tiles, mode_count, lon, LANES), outgoing, rate, scale, shape
     )
-    gradient = control + response
+    gradient = plus(control, response)
 
     evolved = jnp.einsum("cm,smk->sck", forward, arrived[:, :mode_count], precision=HIGHEST)
     live = jnp.arange(slots).astype(jnp.float32) < arrived[:, mode_count, :]

time: 100 us -> 101 us (1.010)
  other arithmetic: 7.36 us -> 0.79 us
  local copies, waits for them, and re-layouts: 6.24 us -> 10.6 us
  Pallas kernels: 81.7 us -> 85.2 us
    add x1 -> x0, other arithmetic: 6.56 us -> none  [shards(): gradient = control + response]
    unnamed x17 -> x21, local copies, waits for them, and re-layouts: 6.23 us -> 10.6 us
    pallas_call x0 -> x1, Pallas kernels: none -> 3.56 us  [plus(): pl.pallas_call(add_kernel, grid=(a.shape[0] // STEP,), in_specs=[block, b...]
where the time goes in v3:
time: 101 us
  Pallas kernels  85.2 us (84%)
  local copies, waits for them, and re-layouts  10.6 us (10%)
  matrix products  3.71 us (4%)
    pallas_call x2, Pallas kernels, smooth(): pl.pallas_call(functools.partial(smooth_kernel, halves), in_specs=[SMEM,...  64.9 us
    pallas_call x1, Pallas kernels, shards(): pl.pallas_call(functools.partial(observe_kernel, lon), in_specs=[SMEM, SM...  16.7 us
    unnamed x21, local copies, waits for them, and re-layouts  10.6 us
    pallas_call x1, Pallas kernels, plus(): pl.pallas_call(add_kernel, grid=(a.shape[0] // STEP,), in_specs=[block, b...  3.56 us

profile of v3, /device:TPU:1, one launch (start us, length us, event | category | flops | bytes accessed | tf_op | source)
XLA Modules:
  0.0 101.1 jit_solution(10114482668269826420)
XLA Ops:
  0.6 0.0 copy-start
  0.6 0.0 copy-start.8
  0.7 0.0 copy-start.5
  0.7 0.8 copy-done
  1.5 0.0 copy-start.6
  1.5 1.0 fusion.18
  2.5 1.5 %convolution_bitcast_fusion.1.parcel_ref = f32[8,64,128]{2,1,0:T(8,128)S(1)} fusion(f32[1,1,8,128,128]{4,3,2,1,0:T(8,128)} %param.13, f32[128,64]{0,1:T(8,128)S(1)} %fusion.18, f32[128]{0:T(128)} %param.12), kind=kOutput, calls=%fused_computation.5 | convolution fusion | flops 100671488 | bytes 819712 | tf_op jit(solution)/shard_map/cm,sck->smk/dot_general | solution.py:348
  4.0 0.7 broadcast_divide_fusion
  4.7 0.1 fusion.9
  4.8 0.0 copy-start.1
  4.8 2.2 %copy-done.1 = f32[64,64,256]{2,1,0:T(8,128)S(1)} copy-done((f32[64,64,256]{2,1,0:T(8,128)S(1)}, f32[64,64,256]{2,1,0:T(8,128)}, u32[]{:S(2)}) %copy-start.1) | copy-done | bytes 4194328
  7.0 33.1 %smooth.1 = (f32[2,64,64,128]{3,2,1,0:T(8,128)S(1)}, f32[8,64,128]{2,1,0:T(8,128)S(1)}) custom-call(f32[64]{0:T(128)S(1)} %get-tuple-element.20.rate_ref, f32[64]{0:T(128)S(1)} %sqrt.3.scale_ref, f32[64,64,256]{2,1,0:T(8,128)S(1)} %copy-done.1, f32[8,64,128]{2,1,0:T(8,128)S(1)} %convolution_bitcast_fusion.1.parcel_ref), custom_call_target="tpu_custom_call" | custom-call | tf_op jit(solution)/shard_map/smooth/pallas_call | solution.py:294
  40.1 0.0 copy-done.8
  40.1 0.2 fusion.6.normal_ref
  40.3 0.0 copy-done.5
  40.3 0.0 copy-done.6
  40.3 0.0 copy-start.7
  40.3 16.7 %observe.1 = (f32[8,72,128]{2,1,0:T(8,128)S(1)}, f32[2,4096,128]{2,1,0:T(8,128)S(1)}) custom-call(s32[1024]{0:T(1024)S(1)} %fusion.14.rows_ref, s32[8]{0:T(128)S(1)} %bitcast.64, s32[8,128]{1,0:T(8,128)S(1)} %bitcast.63, f32[2,4096,128]{2,1,0:T(8,128)S(1)} %bitcast.62, f32[64,64]{1,0:T(8,128)S(1)} %fusion.6.normal_ref, ...), custom_call_target="tpu_custom_call" | custom-call | tf_op jit(solution)/shard_map/observe/pallas_call | solution.py:355
  57.0 31.8 %smooth_back.1 = (f32[64,64,256]{2,1,0:T(8,128)S(1)}, f32[8,72,128]{2,1,0:T(8,128)S(1)}) custom-call(f32[64]{0:T(128)S(1)} %get-tuple-element.20.rate_ref, f32[64]{0:T(128)S(1)} %sqrt.3.scale_ref, f32[2,64,64,128]{3,2,1,0:T(8,128)S(1)} %bitcast.61, f32[8,72,128]{2,1,0:T(8,128)S(1)} %get-tuple-element.11.parcel_ref), custom_call_target="tpu_custom_call" | custom-call | tf_op jit(solution)/shard_map/smooth_back/pallas_call | solution.py:294
  88.9 0.0 copy-start.3
  88.9 2.0 %copy-done.3 = f32[64,64,256]{2,1,0:T(8,128)} copy-done((f32[64,64,256]{2,1,0:T(8,128)}, f32[64,64,256]{2,1,0:T(8,128)S(1)}, u32[]{:S(2)}) %copy-start.3) | copy-done | bytes 4194328
  90.9 0.0 copy-done.7
  90.9 0.2 copy.16
  91.2 1.0 %fusion.3 = f32[1,1,8,128,128]{3,4,2,1,0:T(8,128)S(1)} fusion(f32[1,1,8,128,128]{3,4,2,1,0:T(8,128)S(1)} %copy.16, f32[8,72,128]{2,1,0:T(8,128)S(1)} %get-tuple-element.13, f32[128]{0:T(128)S(1)} %copy-done.8, pred[8,128]{1,0:T(8,128)(4,1)S(1)} %bitcast.65, f32[128,64]{0,1:T(8,128)S(1)} %fusion.18), kind=kOutput, calls=%fused_computation.4 | convolution fusion | flops 101056512 | bytes 1345024 | tf_op jit(solution)/shard_map/cm,smk->sck/dot_general | solution.py:376
  92.2 1.0 copy.18
  93.2 0.0 copy-start.2
  93.2 2.2 %copy-done.2 = f32[64,64,256]{2,1,0:T(8,128)S(1)} copy-done((f32[64,64,256]{2,1,0:T(8,128)S(1)}, f32[64,64,256]{2,1,0:T(8,128)}, u32[]{:S(2)}) %copy-start.2) | copy-done | bytes 4194328
  95.4 0.0 copy-start.4
  95.4 2.2 %copy-done.4 = f32[64,64,256]{2,1,0:T(8,128)S(1)} copy-done((f32[64,64,256]{2,1,0:T(8,128)S(1)}, f32[64,64,256]{2,1,0:T(8,128)}, u32[]{:S(2)}) %copy-start.4) | copy-done | bytes 4194328
  97.6 3.6 %plus.1 = f32[64,64,256]{2,1,0:T(8,128)} custom-call(f32[64,64,256]{2,1,0:T(8,128)S(1)} %copy-done.2, f32[64,64,256]{2,1,0:T(8,128)S(1)} %copy-done.4), custom_call_target="tpu_custom_call" | custom-call | tf_op jit(solution)/shard_map/plus/pallas_call | solution.py:320
  (6 shorter events, 0.0 us)
Async XLA Ops:
  0.6 0.8 copy-start
  0.6 39.4 %copy-start.8 = (f32[128]{0:T(128)S(1)}, f32[128]{0:T(128)}, u32[]{:S(2)}) copy-start(f32[128]{0:T(128)} %param.12) | copy-start | bytes 1540
  0.7 39.6 %copy-start.5 = (s32[1,1,8,128]{3,2,1,0:T(8,128)S(1)}, s32[1,1,8,128]{3,2,1,0:T(8,128)}, u32[]{:S(2)}) copy-start(s32[1,1,8,128]{3,2,1,0:T(8,128)} %param.14) | copy-start | bytes 12292
  1.5 38.8 %copy-start.6 = (s32[1,1,8]{2,1,0:T(1,128)S(1)}, s32[1,1,8]{2,1,0:T(1,128)}, u32[]{:S(2)}) copy-start(s32[1,1,8]{2,1,0:T(1,128)} %param.15) | copy-start | bytes 100
  4.8 2.2 %copy-start.1 = (f32[64,64,256]{2,1,0:T(8,128)S(1)}, f32[64,64,256]{2,1,0:T(8,128)}, u32[]{:S(2)}) copy-start(f32[64,64,256]{2,1,0:T(8,128)} %a_ref.1) | copy-start | bytes 12582916
  40.3 50.6 %copy-start.7 = (f32[1,1,8,128,128]{4,3,2,1,0:T(8,128)S(1)}, f32[1,1,8,128,128]{4,3,2,1,0:T(8,128)}, u32[]{:S(2)}) copy-start(f32[1,1,8,128,128]{4,3,2,1,0:T(8,128)} %param.13) | copy-start | bytes 1572868
  88.9 2.0 %copy-start.3 = (f32[64,64,256]{2,1,0:T(8,128)}, f32[64,64,256]{2,1,0:T(8,128)S(1)}, u32[]{:S(2)}) copy-start(f32[64,64,256]{2,1,0:T(8,128)S(1)} %get-tuple-element.12.b_ref) | copy-start | bytes 12582916
  93.2 2.2 %copy-start.2 = (f32[64,64,256]{2,1,0:T(8,128)S(1)}, f32[64,64,256]{2,1,0:T(8,128)}, u32[]{:S(2)}) copy-start(f32[64,64,256]{2,1,0:T(8,128)} %a_ref.1) | copy-start | bytes 12582916
  95.4 2.2 %copy-start.4 = (f32[64,64,256]{2,1,0:T(8,128)S(1)}, f32[64,64,256]{2,1,0:T(8,128)}, u32[]{:S(2)}) copy-start(f32[64,64,256]{2,1,0:T(8,128)} %copy-done.3) | copy-start | bytes 12582916
